TPU v7x, 256 devices: a whole 4x4x8 slice. The times are simulated.
256 devices in a mesh: frame: 32 (over y_lo, z, core), space: 8 (over x, y_hi).
Axes of the slice: x: 4, y: 4 (y_hi: 2, y_lo: 2; y = y_hi * 2 + y_lo), z: 8, core: 2. Of those that a mesh axis runs over, the one named last changes fastest.
Arguments:
- latents: float32 [64, 16, 1024], P('frame', None, 'space'), may hold values from -6 to 6
- time_index: int32 [64], P('frame'), may hold values from 0 to 127, as said below
- fresh_noise: float32 [16, 1024], P(None, 'space'), may hold values from -6 to 6
- modulation_table: bfloat16 [128, 8, 1152], replicated, may hold values from -3 to 3
- embed_weight: bfloat16 [16, 1152], replicated, may hold values from -1.5 to 1.5
- spatial_qkv: bfloat16 [1152, 3456], P(None, 'space'), may hold values from -0.1875 to 0.1875
- spatial_out: bfloat16 [1152, 1152], P('space'), may hold values from -0.1875 to 0.1875
- temporal_qkv: bfloat16 [1152, 3456], P(None, 'space'), may hold values from -0.1875 to 0.1875
- temporal_out: bfloat16 [1152, 1152], P('space'), may hold values from -0.1875 to 0.1875
- final_weight: bfloat16 [1152, 16], replicated, may hold values from -0.1875 to 0.1875
- spatial_gain: float32 [2, 72], replicated, may hold values from 1 to 2.5
- temporal_gain: float32 [2, 72], replicated, may hold values from 1 to 2.5
Outputs:
- velocity: float32 [64, 16, 1024], P('frame', None, 'space')
- queue_next: float32 [64, 16, 1024], P('frame', None, 'space')
Inputs may be any that keep to these rules, and one draw needn't show every extreme that they name: `time_index`: 64 distinct indices rising along the queue; the first is 0 and the last is 127.
All inputs are finite; a program needn't handle non-finite values.
Results may differ from a plain program's by a relative error of at most 0.02.
Values may be sent and summed in bfloat16 or wider, within the bound.
A program may use at most 128 MiB of HBM per device.

v0:
```python
import jax
import jax.numpy as jnp
from jax import lax
from jax.sharding import PartitionSpec as P

HEAD_DIM = 72


time_shift = 3.0
norm_eps = 1e-06


def passed_along(block, axis, distance):
    devices = range(lax.axis_size(axis))
    route = [(i - distance, i) for i in devices if i - distance in devices]
    return lax.ppermute(block, axis, route)


def level(index, total):
    fraction = index.astype(jnp.float32) / total
    return time_shift * fraction / (1.0 + (time_shift - 1.0) * fraction)


def layer_norm(values):
    center = values - jnp.mean(values, axis=-1, keepdims=True)
    spread = jnp.mean(center * center, axis=-1, keepdims=True)
    return center / jnp.sqrt(spread + norm_eps)


def head_norm(values, gain):
    power = jnp.mean(values * values, axis=-1, keepdims=True)
    return values / jnp.sqrt(power + norm_eps) * gain


def project(ready, weight, gain):
    frames, tokens, width = ready.shape
    heads = weight.shape[1] // (3 * HEAD_DIM)
    projected = jnp.dot(
        ready.reshape(frames * tokens, width), weight, preferred_element_type=jnp.float32
    )
    projected = projected.reshape(frames, tokens, heads, 3, HEAD_DIM)
    query = head_norm(projected[:, :, :, 0], gain[0]).astype(jnp.bfloat16)
    keys = head_norm(projected[:, :, :, 1], gain[1]).astype(jnp.bfloat16)
    values = projected[:, :, :, 2].astype(jnp.bfloat16)
    return jnp.stack((query, keys, values), axis=3)


def attend_tokens(stacked):
    score_scale = HEAD_DIM ** (-0.5)
    scores = (
        jnp.einsum(
            "qhc,khc->hqk", stacked[:, :, 0], stacked[:, :, 1], preferred_element_type=jnp.float32
        )
        * score_scale
    )
    weights = jnp.exp(scores)
    total = jnp.sum(weights, axis=-1)
    weighted = jnp.einsum(
        "hqk,khc->qhc",
        weights.astype(jnp.bfloat16),
        stacked[:, :, 2],
        preferred_element_type=jnp.float32,
    )
    return (weighted / jnp.transpose(total)[:, :, None]).astype(jnp.bfloat16)


def attend_queue(packed):
    score_scale = HEAD_DIM ** (-0.5)
    received = lax.all_to_all(packed, "frame", split_axis=1, concat_axis=0, tiled=True)
    all_frames = received.shape[0]
    count = received.shape[2]
    heads = received.shape[3] // (3 * HEAD_DIM)
    split = received.reshape(all_frames, count, heads, 3, HEAD_DIM)
    scores = (
        jnp.einsum(
            "fghc,kghc->ghfk",
            split[:, :, :, 0],
            split[:, :, :, 1],
            preferred_element_type=jnp.float32,
        )
        * score_scale
    )
    weights = jnp.exp(scores)
    total = jnp.sum(weights, axis=-1)
    weighted = jnp.einsum(
        "ghfk,kghc->fghc",
        weights.astype(jnp.bfloat16),
        split[:, :, :, 2],
        preferred_element_type=jnp.float32,
    )
    result = (weighted / jnp.transpose(total, (2, 0, 1))[..., None]).astype(jnp.bfloat16)
    result = result.reshape(all_frames, 1, count, heads * HEAD_DIM)
    return lax.all_to_all(result, "frame", split_axis=0, concat_axis=1, tiled=True)


def local(
    latents,
    time_index,
    fresh_noise,
    modulation_table,
    embed_weight,
    spatial_qkv,
    spatial_out,
    temporal_qkv,
    temporal_out,
    final_weight,
    spatial_gain,
    temporal_gain,
):
    frames_here, patch_size, tokens_here = latents.shape
    width = embed_weight.shape[1]
    steps_total = modulation_table.shape[0]
    frame_count = lax.axis_size("frame")
    picker = (time_index[:, None] == jnp.arange(steps_total, dtype=jnp.int32)[None, :]).astype(
        jnp.bfloat16
    )
    modulation = jnp.dot(
        picker, modulation_table.reshape(steps_total, 8 * width), preferred_element_type=jnp.float32
    ).reshape(frames_here, 8, width)
    tokens_in = latents.astype(jnp.bfloat16).astype(jnp.float32)
    hidden = jnp.einsum("fct,cd->ftd", tokens_in, embed_weight.astype(jnp.float32))
    ready = (layer_norm(hidden) * (1.0 + modulation[:, None, 1]) + modulation[:, None, 0]).astype(
        jnp.bfloat16
    )
    gathered = project(
        lax.all_gather(ready, "space", axis=1, tiled=True), spatial_qkv, spatial_gain
    )
    all_tokens, local_heads = (gathered.shape[1], gathered.shape[2])
    attended = lax.map(attend_tokens, gathered)
    arranged = jnp.transpose(
        attended.reshape(frames_here, all_tokens, local_heads * HEAD_DIM), (1, 0, 2)
    )
    count = tokens_here * lax.axis_size("space")
    rows = arranged
    term = jnp.dot(
        rows.reshape(count * frames_here, local_heads * HEAD_DIM),
        spatial_out,
        preferred_element_type=jnp.float32,
    )
    summed = lax.psum_scatter(
        term.reshape(count, frames_here, width).astype(jnp.bfloat16),
        "space",
        scatter_dimension=0,
        tiled=True,
    ).astype(jnp.float32)
    output = jnp.transpose(summed, (1, 0, 2))
    hidden = hidden + modulation[:, None, 2] * output
    ready = (layer_norm(hidden) * (1.0 + modulation[:, None, 4]) + modulation[:, None, 3]).astype(
        jnp.bfloat16
    )
    gathered = project(
        lax.all_gather(ready, "space", axis=1, tiled=True), temporal_qkv, temporal_gain
    )
    packed = gathered.reshape(
        frames_here, frame_count, all_tokens // frame_count, local_heads * 3 * HEAD_DIM
    )
    attended = attend_queue(packed)
    attended = attended.reshape(frames_here, all_tokens, local_heads * HEAD_DIM)
    arranged = jnp.transpose(attended, (1, 0, 2))
    count = tokens_here * lax.axis_size("space")
    rows = arranged
    term = jnp.dot(
        rows.reshape(count * frames_here, local_heads * HEAD_DIM),
        temporal_out,
        preferred_element_type=jnp.float32,
    )
    summed = lax.psum_scatter(
        term.reshape(count, frames_here, width).astype(jnp.bfloat16),
        "space",
        scatter_dimension=0,
        tiled=True,
    ).astype(jnp.float32)
    hidden = hidden + modulation[:, None, 5] * jnp.transpose(summed, (1, 0, 2))
    ready = (layer_norm(hidden) * (1.0 + modulation[:, None, 7]) + modulation[:, None, 6]).astype(
        jnp.bfloat16
    )
    predicted = jnp.dot(
        ready.reshape(frames_here * tokens_here, width),
        final_weight,
        preferred_element_type=jnp.float32,
    )
    velocity = jnp.transpose(predicted.reshape(frames_here, tokens_here, patch_size), (0, 2, 1))
    step_size = level(time_index + 1, steps_total) - level(time_index, steps_total)
    updated = latents - step_size[:, None, None] * velocity
    incoming = passed_along(updated[0:1], "frame", -1)
    is_tail = lax.axis_index("frame") == frame_count - 1
    tail_frame = jnp.where(is_tail, fresh_noise[None], incoming)
    queue_next = jnp.concatenate([updated[1:], tail_frame], axis=0)
    return (velocity, queue_next)


def solution(mesh):
    return jax.shard_map(
        local,
        mesh=mesh,
        in_specs=(
            P("frame", None, "space"),
            P("frame"),
            P(None, "space"),
            P(),
            P(),
            P(None, "space"),
            P("space", None),
            P(None, "space"),
            P("space", None),
            P(),
            P(),
            P(),
        ),
        out_specs=(P("frame", None, "space"), P("frame", None, "space")),
        check_vma=False,
    )
```

profile of v0, /device:TPU:1, one launch (start us, length us, event | category | flops | bytes accessed | tf_op | source)
XLA Modules:
  0.0 547.6 jit_solution(2124106254169931190)
XLA Ops:
  7.2 3.6 copy.53
  10.8 3.0 copy.31
  13.9 0.7 fusion.43
  14.7 0.4 fusion.52
  15.2 0.3 multiply_reduce_fusion.6
  15.4 0.8 copy-done.2
  16.2 1.1 add_convert_fusion.2
  17.4 84.4 %all-gather.3.cloned.1.call-done = bf16[2,1024,1152]{2,1,0:T(8,128)(2,1)} async-done(((bf16[2,128,1152]{2,1,0:T(8,128)(2,1)}), bf16[2,1024,1152]{2,1,0:T(8,128)(2,1)}) %all-gather.3.cloned.1.call-update) | async-done | bytes 4718608 | tf_op jit(solution)/shard_map/all_gather | solution.py:126
  101.8 4.8 fusion.24
  106.7 0.3 multiply_reduce_fusion.5
  107.1 0.5 multiply_convert_fusion.3
  107.8 5.8 %while.10 = (s32[]{:T(128)}, bf16[2,1024,2,72]{1,3,2,0:T(8,128)(2,1)S(1)}, bf16[2,1024,2,3,72]{1,4,3,2,0:T(8,128)(2,1)S(1)}, s32[]{:T(128)}) while((s32[]{:T(128)}, bf16[2,1024,2,72]{1,3,2,0:T(8,128)(2,1)S(1)}, bf16[2,1024,2,3,72]{1,4,3,2,0:T(8,128)(2,1)S(1)}, s32[]{:T(128)}) %tuple.49), condition=%wide.region_6.7_spmd, body=%wide.region_4.6_spmd.sunk | while | flops 612661248 | bytes 19742780 | solution.py:129
  107.9 1.4 fusion.61
  109.3 1.4 fusion.62
  110.8 1.4 fusion.61
  112.3 1.4 fusion.62
  113.7 4.7 convolution_convert_fusion.1
  118.4 90.8 %reduce-scatter.3.cloned.1.call-done = bf16[128,2,1152]{2,0,1:T(8,128)(2,1)} async-done(((bf16[1024,2,1152]{2,0,1:T(8,128)(2,1)}), bf16[128,2,1152]{2,0,1:T(8,128)(2,1)}) %reduce-scatter.3.cloned.1.call-update) | async-done | bytes 589840 | tf_op jit(solution)/shard_map/reduce_scatter | solution.py:140
  209.2 1.3 fusion.49
  210.6 0.3 multiply_reduce_fusion.3
  210.9 1.1 add_convert_fusion.1
  212.0 0.2 reduce-scatter.5.cloned.1.call-start
  212.2 80.6 %all-gather.5.cloned.1.call-done = bf16[2,1024,1152]{2,1,0:T(8,128)(2,1)} async-done(((bf16[2,128,1152]{2,1,0:T(8,128)(2,1)}), bf16[2,1024,1152]{2,1,0:T(8,128)(2,1)}) %all-gather.5.cloned.1.call-update) | async-done | bytes 4718608 | tf_op jit(solution)/shard_map/all_gather | solution.py:152
  292.9 4.8 fusion.22
  297.7 0.3 multiply_reduce_fusion.2
  298.2 0.5 multiply_convert_fusion.1
  298.7 1.5 pad_maximum_fusion.1
  300.2 9.2 %reshape.143 = bf16[2,32,32,432]{2,1,3,0:T(8,128)(2,1)} reshape(bf16[2,1024,2,3,72]{1,4,3,2,0:T(8,128)(2,1)} %pad_maximum_fusion.1) | data formatting | bytes 3538944 | tf_op jit(solution)/shard_map/reshape | solution.py:154
  309.4 8.6 %copy.34 = bf16[2,32,32,432]{3,2,0,1:T(8,128)(2,1)} copy(bf16[2,32,32,432]{2,1,3,0:T(8,128)(2,1)} %reshape.143) | data formatting | bytes 3538944 | tf_op jit(solution)/shard_map/reshape | solution.py:154
  318.0 57.3 %all_to_all.30 = bf16[2,32,32,432]{3,2,0,1:T(8,128)(2,1)} all-to-all(bf16[2,32,32,432]{3,2,0,1:T(8,128)(2,1)} %copy.34), channel_id=1, replica_groups=mesh['frame'=32,'space'=8] {'frame'}, dimensions={1} | all-to-all | bytes 3538944 | tf_op jit(solution)/shard_map/all_to_all | solution.py:69
  375.3 10.5 %reshape.131 = bf16[64,32,2,3,72]{4,3,2,1,0:T(4,128)(2,1)} reshape(bf16[32,2,1,32,432]{4,3,1,0,2:T(8,128)(2,1)} %bitcast.177) | data formatting | bytes 3538944 | tf_op jit(solution)/shard_map/reshape | solution.py:73
  385.8 11.2 %fusion.50 = (bf16[64,32,2,1,72]{4,3,2,1,0:T(2,128)(2,1)S(1)}, bf16[64,32,2,1,72]{4,3,2,1,0:T(2,128)(2,1)S(1)}, bf16[64,32,2,1,72]{4,3,2,1,0:T(2,128)(2,1)S(1)}) fusion(bf16[64,32,2,3,72]{4,3,2,1,0:T(4,128)(2,1)} %reshape.131), kind=kLoop, calls=%fused_computation.98 | loop fusion | bytes 3538944 | tf_op jit(solution)/shard_map/slice | solution.py:88
  397.0 2.7 fusion.27
  399.7 2.1 fusion.26
  401.8 1.1 copy.39
  402.9 1.5 reshape.132
  404.4 32.4 %all_to_all.31 = bf16[64,1,32,144]{3,2,1,0:T(8,128)(2,1)S(1)} all-to-all(bf16[64,1,32,144]{3,2,1,0:T(8,128)(2,1)} %bitcast.178), channel_id=1, replica_groups=mesh['frame'=32,'space'=8] {'frame'}, dimensions={0} | all-to-all | bytes 1179648 | tf_op jit(solution)/shard_map/all_to_all | solution.py:93
  436.9 0.4 copy.42
  437.4 0.5 copy-done.5
  437.9 3.7 convolution_convert_fusion
  441.7 89.4 %reduce-scatter.5.cloned.1.call-done = bf16[128,2,1152]{2,0,1:T(8,128)(2,1)} async-done(((bf16[1024,2,1152]{2,0,1:T(8,128)(2,1)}), bf16[128,2,1152]{2,0,1:T(8,128)(2,1)}) %reduce-scatter.5.cloned.1.call-update) | async-done | bytes 589840 | tf_op jit(solution)/shard_map/reduce_scatter | solution.py:167
  531.1 1.4 fusion.35
  532.5 0.3 multiply_reduce_fusion
  532.9 0.4 copy-done.13
  533.3 1.1 multiply_subtract_fusion
  534.3 3.8 collective-permute-start
  538.1 2.3 collective-permute-done
  540.5 0.6 pad_maximum_fusion.2
  (54 shorter events, 1.0 us)
Async XLA Ops:
  7.2 94.7 %copy-start = (bf16[1152,432]{0,1:T(8,128)(2,1)S(1)}, bf16[1152,432]{0,1:T(8,128)(2,1)}, u32[]{:S(2)}) copy-start(bf16[1152,432]{0,1:T(8,128)(2,1)} %param.19) | copy-start | bytes 2985988
  7.2 94.7 %all-gather.3.cloned.1.call-start = ((), (), s32[]{:S(2)}) async-start(), calls=%async_computation.4 | async-start | bytes 5308416 | tf_op jit(solution)/shard_map/all_gather | solution.py:126
  10.8 3.1 copy-start.11
  13.9 0.8 copy-start.6
  13.9 0.8 copy-start.7
  15.1 1.1 copy-start.2
  16.2 1.2 copy-start.9
  17.3 191.9 %reduce-scatter.3.cloned.1.call-start = ((), (), s32[]{:S(2)}) async-start(), calls=%async_computation.5 | async-start | bytes 5308416 | tf_op jit(solution)/shard_map/reduce_scatter | solution.py:140
  118.4 90.9 %copy-start.3 = (f32[2,128,1152]{2,1,0:T(8,128)S(1)}, f32[2,128,1152]{2,1,0:T(8,128)}, u32[]{:S(2)}) copy-start(f32[2,128,1152]{2,1,0:T(8,128)} %copy-done.2) | copy-start | bytes 3538948
  118.4 174.5 %all-gather.5.cloned.1.call-start = ((), (), s32[]{:S(2)}) async-start(), calls=%async_computation.6 | async-start | bytes 5308416 | tf_op jit(solution)/shard_map/all_gather | solution.py:152
  210.8 1.4 copy-start.10
  210.9 82.0 %copy-start.12 = (bf16[1152,432]{0,1:T(8,128)(2,1)S(1)}, bf16[1152,432]{0,1:T(8,128)(2,1)}, u32[]{:S(2)}) copy-start(bf16[1152,432]{0,1:T(8,128)(2,1)} %param.21) | copy-start | bytes 2985988
  212.0 319.1 %reduce-scatter.5.cloned.1.call-start = ((), (), s32[]{:S(2)}) async-start(), calls=%async_computation.7 | async-start | bytes 5308416 | tf_op jit(solution)/shard_map/reduce_scatter | solution.py:167
  436.9 1.0 copy-start.5
  531.1 1.4 copy-start.4
  532.5 0.8 copy-start.13
  533.3 7.2 %copy-start.8 = (f32[16,128]{1,0:T(8,128)S(1)}, f32[16,128]{1,0:T(8,128)}, u32[]{:S(2)}) copy-start(f32[16,128]{1,0:T(8,128)} %param.16) | copy-start | bytes 24580
  533.3 7.8 %copy-start.1 = (bf16[1152,432]{0,1:T(8,128)(2,1)S(1)}, bf16[1152,432]{0,1:T(8,128)(2,1)}, u32[]{:S(2)}) copy-start(bf16[1152,432]{0,1:T(8,128)(2,1)} %param.19) | copy-start | bytes 2985988
  534.3 6.1 %collective-permute-start = (f32[1,16,128]{2,1,0:T(8,128)S(1)}, f32[1,16,128]{2,1,0:T(8,128)S(1)}, u32[]{:S(2)}, u32[]{:S(2)}) collective-permute-start(f32[1,16,128]{2,1,0:T(8,128)S(1)} %get-tuple-element.59), channel_id=1, source_target_pairs={{8,0},{16,8},{24,16},{32,24},{40,32},{48,40},{56,48},{64,56},{72,6... | collective-permute-start | bytes 24584 | tf_op jit(solution)/shard_map/ppermute | solution.py:16
Sparse Core Ops, SparseCore 0:
  17.4 84.3 all-gather.2
  118.5 90.6 reduce-scatter.2
  212.2 80.6 all-gather.4
  441.8 89.2 reduce-scatter.4
where the time goes:
time: 549 us; the launch traced here: 548 us
  waiting for transfers between devices  348 us (63%)
  blocking collectives  89.7 us (16%)
  local copies, waits for them, and re-layouts  51.3 us (9%)
  matrix products  30.8 us (6%)
  between operations  14.1 us (3%)
  other arithmetic  9.82 us (2%)
    reduce_scatter x2, waiting for transfers between devices, local(): lax.psum_scatter(term.reshape(count, frames_here, width).astype(jnp.bfloa...  180 us
    all_gather x2, waiting for transfers between devices, local(): lax.all_gather(ready, 'space', axis=1, tiled=True)  165 us
    all_to_all x1, blocking collectives, attend_queue(): lax.all_to_all(packed, 'frame', split_axis=1, concat_axis=0, tiled=True)  57.3 us
    all_to_all x1, blocking collectives, attend_queue(): lax.all_to_all(result, 'frame', split_axis=0, concat_axis=1, tiled=True)  32.4 us
    reshape x2, local copies, waits for them, and re-layouts, local(): gathered.reshape(frames_here, frame_count, all_tokens // frame_count, loc...  17.9 us
    slice x1, local copies, waits for them, and re-layouts, attend_queue(): split[:, :, :, 2]  11.2 us
  transfers between devices with their start and end apart: 5, of which 5 were waited for; matrix products, arithmetic and copies ran while one was open for 0% of the time, Pallas kernels for 0%

commit v1 on v0

v1 whole, which is shorter than its diff:
```python
import jax
import jax.numpy as jnp
from jax import lax
from jax.experimental import pallas as pl
from jax.experimental.pallas import tpu as pltpu
from jax.sharding import PartitionSpec as P

HD = 72
D = 1152
NF = 32
NS = 8
STEPS = 128
PATCH = 16
TOK = 1024
OWN = 128
SUB = 4
SHARD = 768
QUARTER = SHARD // 4
OUT_S, QKV_T, OUT_T = 0, 144, 576
ROWS = 2 * SUB * NF
WIDE = 640
EPS = 1e-6
LOG2E = 1.4426950408889634
SCORE = HD ** -0.5 * LOG2E
BF = jnp.bfloat16
F32 = jnp.float32

NN = (((1,), (0,)), ((), ()))
NT = (((1,), (1,)), ((), ()))


def dot(a, b, dims=NN, precision=None):
    return lax.dot_general(a, b, dims, preferred_element_type=F32, precision=precision)


def iota(shape, axis):
    return lax.broadcasted_iota(jnp.int32, shape, axis)


def split2(a):
    high = a.astype(BF)
    return high, (a - high.astype(F32)).astype(BF)


def split3(a):
    high = a.astype(BF)
    rest = a - high.astype(F32)
    mid = rest.astype(BF)
    return high, mid, (rest - mid.astype(F32)).astype(BF)


def layer_norm(a):
    center = a - jnp.mean(a, axis=-1, keepdims=True)
    spread = jnp.mean(center * center, axis=-1, keepdims=True)
    return center * lax.rsqrt(spread + EPS)


def head_norm(a, gain):
    return a * lax.rsqrt(jnp.mean(a * a, axis=0, keepdims=True) + EPS) * gain


def level(index):
    fraction = index * (1.0 / STEPS)
    return 3.0 * fraction / (1.0 + 2.0 * fraction)


def kernel(
    latents, steps, noise, table, embed, qkv_s, out_s, qkv_t, out_t, final, gains,
    velocity, queue,
    weights, lat_send, lat_all, lat_next, step_rows, qb, kb, vb, att_f, att, att_in, send, recv,
    mods, proj, att_t, vel_send, vel_recv,
    lat_ssem, lat_rsem, next_sem, step_ssem, step_rsem, dir_ssem, dir_rsem, core_ssem, core_rsem,
    att_ssem, att_rsem, row_ssem, row_rsem, vel_ssem, vel_rsem, own_sem,
):
    f = lax.axis_index("frame")
    s = lax.axis_index("space")
    c = f % 2
    yl = f // 16
    x = s // 2
    yh = s % 2

    def frame_peer(k):
        return lax.rem(f + k, NF)

    def space_peer(k):
        return lax.rem(s + k, NS)

    step = 1 - 2 * c
    to_x = (f, lax.rem(x + step + 4, 4) * 2 + yh)
    to_core = (f + step, s)
    to_cross = (lax.rem(f + 16, NF), 2 * x + 1 - yh)
    to_side = (lax.rem(f + 16, NF), s)

    barrier = pltpu.get_barrier_semaphore()

    def greet(target):
        pl.semaphore_signal(barrier, inc=1, device_id=target, device_id_type=pl.DeviceIdType.MESH)

    @pl.loop(1, NF)
    def _(k):
        greet((frame_peer(k), s))

    @pl.loop(1, NS)
    def _(k):
        greet((f, space_peer(k)))

    greet(to_cross)

    def push(src, dst, ssem, rsem, target):
        return pltpu.make_async_remote_copy(
            src_ref=src, dst_ref=dst, send_sem=ssem, recv_sem=rsem,
            device_id=target, device_id_type=pl.DeviceIdType.MESH,
        )

    for j in range(2):
        lat_send[j] = latents[j].astype(BF)
    weights[s, OUT_S:QKV_T, :] = out_s[...]
    weights[s, OUT_T : OUT_T + 144, :] = out_t[...]
    weights[s, OUT_T + 144 :, :] = jnp.zeros((SHARD - OUT_T - 144, D), BF)
    eye = (iota((432, 432), 0) == iota((432, 432), 1)).astype(BF)
    weights[s, QKV_T:OUT_T, :] = dot(eye, qkv_t[...], NT).astype(BF)
    half = iota((8, 128), 0) < SUB
    own_steps = jnp.where(half, steps[0], steps[1]).astype(F32)
    step_rows[pl.ds(pl.multiple_of(f * 8, 8), 8), :] = own_steps
    step_rows[ROWS:, :] = jnp.zeros((8, 128), F32)
    vel_send[...] = jnp.zeros(vel_send.shape, F32)

    pl.semaphore_wait(barrier, NF + NS - 1)

    def lat_copy(k):
        return push(lat_send, lat_all.at[s], lat_ssem.at[k], lat_rsem.at[s], (f, space_peer(k)))

    def lat_wait(k):
        origin = space_peer(k)
        push(lat_send, lat_all.at[origin], lat_ssem.at[k], lat_rsem.at[origin], (f, origin)).wait_recv()

    def next_copy():
        return push(latents.at[0], lat_next, next_sem.at[0], next_sem.at[1], (frame_peer(NF - 1), s))

    def step_copy(k, row):
        rows = pl.ds(pl.multiple_of(row * 8, 8), 8)
        return push(
            step_rows.at[rows], step_rows.at[rows], step_ssem.at[k], step_rsem.at[row], (frame_peer(k), s)
        )

    @pl.loop(1, NS)
    def _(k):
        lat_copy(k).start()

    own_lat = pltpu.make_async_copy(lat_send, lat_all.at[s], own_sem.at[0])
    own_lat.start()

    def block(i, who):
        turn = 1 - 2 * who
        before = lax.rem(x - turn + 4, 4)
        after = lax.rem(x + turn + 4, 4)
        far = lax.rem(x + 2, 4)
        q = 2 * yl + who
        r = 2 * (1 - yl) + who
        if i < 4:
            return before * 2 + yh, (q, 2 * yl + 1 - who, r, 2 * (1 - yl) + 1 - who)[i]
        if i < 6:
            return far * 2 + yh, (q, r)[i - 4]
        across = (x, before, after, far)[(i - 6) % 4] * 2 + 1 - yh
        return across, (r if i < 10 else q)

    def place(share, quarter):
        return weights.at[share, pl.ds(pl.multiple_of(quarter * QUARTER, QUARTER), QUARTER), :]

    def hop(i, share, quarter):
        target = to_x if i < 6 else to_cross if i < 10 else to_side
        spot = place(share, quarter)
        return push(spot, spot, dir_ssem.at[i], dir_rsem.at[i], target)

    def hop_source(i):
        q = 2 * yl + c
        r = 2 * (1 - yl) + c
        if i < 4:
            return s, (q, 2 * yl + 1 - c, r, 2 * (1 - yl) + 1 - c)[i]
        if i < 6:
            return block((0, 2)[i - 4], c)
        if i < 10:
            near = (x, lax.rem(x - step + 4, 4), lax.rem(x + step + 4, 4), lax.rem(x + 2, 4))[i - 6]
            return near * 2 + yh, q
        return block(i - 4, c)

    def hop_start(i):
        hop(i, *hop_source(i)).start()

    def core_copy(i, who):
        spot = place(*block(i, who))
        return push(spot, spot, core_ssem.at[i], core_rsem.at[i], to_core)

    def take(i, *then):
        hop(i, *block(i, c)).wait_recv()
        core_copy(i, c).start()
        for j in then:
            hop_start(j)

    def take_core(i, *then):
        core_copy(i, 1 - c).wait_recv()
        for j in then:
            hop_start(j)

    hop_start(0)
    hop_start(6)
    hop_start(1)

    @pl.loop(1, NF)
    def _(k):
        step_copy(k, f).start()

    next_copy().start()
    hop_start(2)
    hop_start(3)

    base = embed[...].astype(F32)
    center = base - jnp.mean(base, axis=1, keepdims=True)
    gram = dot(center, center, NT, lax.Precision.HIGHEST) * (1.0 / D)
    gram3 = jnp.concatenate(split3(gram), axis=1)
    pick_row = iota((8, 8 * STEPS), 0)
    pick = jnp.zeros((8, 8 * STEPS), jnp.bool_)
    for j in range(2):
        for kind in range(2):
            pick |= (pick_row == 2 * j + kind) & (iota((8, 8 * STEPS), 1) == steps[j] * 8 + kind)
    own_mods = dot(pick.astype(BF), table[...])
    parts = []
    for j in range(2):
        parts.extend(split2(center * (1.0 + own_mods[2 * j + 1 : 2 * j + 2, :])))
    parts.extend(split2(own_mods))
    stack = jnp.concatenate(parts, axis=0)
    qkv_s_t = dot(eye, qkv_s[...], NT).astype(BF)
    mixed = dot(qkv_s_t, stack, NT)

    own_lat.wait()

    @pl.loop(1, NS)
    def _(k):
        lat_wait(k)

    def project_frame(j):
        lat = jnp.concatenate([lat_all[i, j] for i in range(NS)], axis=1)
        lat32 = lat.astype(F32)
        spread = jnp.sum(lat32 * dot(gram3, jnp.concatenate([lat] * 3, axis=0)), axis=0, keepdims=True)
        rstd = lax.rsqrt(jnp.maximum(spread, 0.0) + EPS)
        matrix = mixed[:, 32 * j : 32 * j + 16] + mixed[:, 32 * j + 16 : 32 * j + 32]
        shift = mixed[:, 64 + 2 * j : 65 + 2 * j] + mixed[:, 72 + 2 * j : 73 + 2 * j]
        matrix2 = jnp.concatenate(split2(matrix), axis=1)
        projected = dot(matrix2, jnp.concatenate([lat] * 2, axis=0)) * rstd + shift
        ones = (iota((8, TOK), 0) == 0).astype(F32)
        for h in range(2):
            at = h * 3 * HD
            query = head_norm(projected[at : at + HD], gains[:, 0:1]) * SCORE
            keys = head_norm(projected[at + HD : at + 2 * HD], gains[:, 1:2])
            values = projected[at + 2 * HD : at + 3 * HD]
            qb[h] = query.astype(BF)
            kb[h] = keys.T.astype(BF)
            vb[h] = jnp.concatenate([values, ones], axis=0).astype(BF)

    def attend_frame(j):
        chunk = 256

        @pl.loop(0, 2 * TOK // chunk)
        def _(i):
            h = i // (TOK // chunk)
            columns = pl.ds(pl.multiple_of(i % (TOK // chunk) * chunk, chunk), chunk)
            scores = dot(kb[h], qb[h, :, columns])
            weighted = dot(vb[h], jnp.exp2(scores).astype(BF))
            att_f[pl.ds(pl.multiple_of(h * HD, 8), HD), columns] = weighted[:HD] / weighted[HD : HD + 1]

        att[j] = att_f[...].astype(BF)

    def share_rows(share):
        return pl.ds(pl.multiple_of(share * 144, 16), 144)

    def share_columns(share):
        return pl.ds(pl.multiple_of(share * OWN, OWN), OWN)

    def att_copy(j, k):
        peer = space_peer(k)
        return push(
            att.at[j, :, share_columns(peer)], att_in.at[j, share_rows(s), :],
            att_ssem.at[j, k], att_rsem.at[j, s], (f, peer),
        )

    def att_wait(j, k):
        origin = space_peer(k)
        push(
            att.at[j, :, share_columns(origin)], att_in.at[j, share_rows(origin), :],
            att_ssem.at[j, k], att_rsem.at[j, origin], (f, origin),
        ).wait_recv()

    def att_own(j):
        return pltpu.make_async_copy(
            att.at[j, :, share_columns(s)], att_in.at[j, share_rows(s), :], own_sem.at[1 + j]
        )

    for j in range(2):
        project_frame(j)
        attend_frame(j)

        @pl.loop(1, NS)
        def _(k):
            att_copy(j, k).start()

        att_own(j).start()
        if j == 0:
            take(0, 4, 7)
        else:
            take(6, 10)
            take(1)
            take_core(1, 8)

    for j in range(2):
        att_own(j).wait()

        @pl.loop(1, NS)
        def _(k):
            att_wait(j, k)

    row, column = iota((16 * NF, 2 * OWN), 0), iota((16 * NF, 2 * OWN), 1)
    matching = column == row % 8 // SUB * OWN + row // 16 * SUB + row % SUB
    upper = row // 8 % 2 == 0
    own_lats = jnp.concatenate([lat_send[0], lat_send[1]], axis=1)
    tail = jnp.concatenate([own_lats, jnp.zeros((WIDE - D // 2 - PATCH, 2 * OWN), BF)], axis=0)
    both = jnp.concatenate([att_in[0], att_in[1]], axis=1)
    gathered = jnp.zeros((16 * NF, WIDE), F32)
    for h in range(2):
        piece = jnp.concatenate([both[h * (D // 2) : (h + 1) * (D // 2)], tail], axis=0)
        gathered += dot((matching & (upper == (h == 0))).astype(BF), piece, NT)
    send[...] = gathered.astype(BF)

    def row_copy(k):
        peer = frame_peer(k)
        return push(
            send.at[pl.ds(pl.multiple_of(peer * 16, 16), 16), :],
            recv.at[pl.ds(pl.multiple_of(f * 16, 16), 16), :],
            row_ssem.at[k], row_rsem.at[f], (peer, s),
        )

    def row_wait(k):
        origin = frame_peer(k)
        rows = pl.ds(pl.multiple_of(origin * 16, 16), 16)
        push(send.at[rows, :], recv.at[rows, :], row_ssem.at[k], row_rsem.at[origin], (origin, s)).wait_recv()

    @pl.loop(1, NF)
    def _(k):
        row_copy(k).start()

    own_rows = pl.ds(pl.multiple_of(f * 16, 16), 16)
    own_copy = pltpu.make_async_copy(send.at[own_rows, :], recv.at[own_rows, :], own_sem.at[3])
    own_copy.start()

    @pl.loop(1, NF)
    def _(k):
        step_copy(k, frame_peer(k)).wait_recv()

    wanted = jnp.concatenate([step_rows[0:ROWS, :]] * 8, axis=1) * 8.0
    slots = iota((ROWS, 8 * STEPS), 1).astype(F32)
    for kind in range(6):
        mods[kind] = dot((wanted + (kind + 2.0) == slots).astype(BF), table[...])

    take(2, 5)
    take(3)
    take(4, 9)
    take(7, 11)
    take(5)
    take(10)
    take(8, 12)
    take(11)
    take(9, 13)

    own_copy.wait()

    @pl.loop(1, NF)
    def _(k):
        row_wait(k)

    take(12)
    take(13)

    for i in (0, 2, 3, 4, 5, 6, 7, 8, 9, 10, 11, 12, 13):
        take_core(i)

    row, column = iota((ROWS, 16 * NF), 0), iota((ROWS, 16 * NF), 1)
    halves = [
        dot((column == row // 8 * 16 + h * 8 + row % 8).astype(BF), recv[...]) for h in range(2)
    ]
    hidden = dot(halves[0][:, D // 2 : D // 2 + PATCH].astype(BF), embed[...])
    output = jnp.zeros((ROWS, D), F32)
    for i in range(NS):
        at = i % 4 * 144
        output += dot(halves[i // 4][:, at : at + 144].astype(BF), weights[i, OUT_S:QKV_T, :])
    hidden += mods[0] * output

    ready = (layer_norm(hidden) * (1.0 + mods[2]) + mods[1]).astype(BF)
    for i in range(NS):
        proj[i] = dot(weights[i, QKV_T:OUT_T, :], ready, NT)
    same = iota((ROWS, ROWS), 0) % SUB == iota((ROWS, ROWS), 1) % SUB
    ones = (iota((8, ROWS), 0) == 0).astype(F32)

    @pl.loop(0, 2 * NS)
    def _(i):
        share, at = i // 2, pl.multiple_of(i % 2 * 3 * HD, 8)
        query = head_norm(proj[share, pl.ds(at, HD), :], gains[:, 2:3]) * SCORE
        keys = head_norm(proj[share, pl.ds(at + HD, HD), :], gains[:, 3:4])
        values = jnp.concatenate([proj[share, pl.ds(at + 2 * HD, HD), :], ones], axis=0).astype(BF)
        scores = dot(keys.T.astype(BF), query.astype(BF))
        weighted = dot(values, jnp.where(same, jnp.exp2(scores), 0.0).astype(BF))
        att_t[pl.ds(pl.multiple_of(i * HD, 8), HD), :] = weighted[:HD] / weighted[HD : HD + 1]

    output = jnp.zeros((ROWS, D), F32)
    for i in range(NS):
        output += dot(att_t[144 * i : 144 * i + 144, :].T.astype(BF), weights[i, OUT_T : OUT_T + 144, :])
    hidden += mods[3] * output
    ready = (layer_norm(hidden) * (1.0 + mods[5]) + mods[4]).astype(BF)
    vel_send[0:ROWS, 0:PATCH] = dot(ready, final[...])

    def vel_copy(k):
        peer = frame_peer(k)
        return push(
            vel_send.at[pl.ds(pl.multiple_of(peer * 8, 8), 16), :], vel_recv.at[f],
            vel_ssem.at[k], vel_rsem.at[f], (peer, s),
        )

    def vel_wait(k):
        origin = frame_peer(k)
        push(
            vel_send.at[pl.ds(pl.multiple_of(origin * 8, 8), 16), :], vel_recv.at[origin],
            vel_ssem.at[k], vel_rsem.at[origin], (origin, s),
        ).wait_recv()

    @pl.loop(1, NF)
    def _(k):
        vel_copy(k).start()

    own_vel = pltpu.make_async_copy(
        vel_send.at[pl.ds(pl.multiple_of(f * 8, 8), 16), :], vel_recv.at[f], own_sem.at[4]
    )
    own_vel.start()
    next_copy().wait_recv()
    own_vel.wait()

    @pl.loop(1, NF)
    def _(k):
        vel_wait(k)

    turned = vel_recv[...].reshape(16 * NF, 128).T[0:PATCH, :]
    turned3 = jnp.concatenate(split3(turned), axis=0)
    row, column = iota((16 * NF, OWN), 0), iota((16 * NF, OWN), 1)
    updated = []
    for j in range(3):
        spread = dot(turned3, (row == column // SUB * 16 + j * SUB + column % SUB).astype(BF))
        found = spread[0:16] + spread[16:32] + spread[32:48]
        index = step_rows[pl.ds(f * 8 + j * SUB, 1), :]
        size = level(index + 1.0) - level(index)
        if j < 2:
            velocity[j] = found
        updated.append((latents[j] if j < 2 else lat_next[...]) - size * found)
    queue[0] = updated[1]
    queue[1] = jnp.where(f == NF - 1, noise[...], updated[2])

    for j in range(2):

        @pl.loop(1, NS)
        def _(k):
            att_copy(j, k).wait_send()

    @pl.loop(1, NS)
    def _(k):
        lat_copy(k).wait_send()

    @pl.loop(1, NF)
    def _(k):
        step_copy(k, f).wait_send()
        row_copy(k).wait_send()
        vel_copy(k).wait_send()

    next_copy().wait_send()
    for i in range(14):
        hop(i, *hop_source(i)).wait_send()
        core_copy(i, c).wait_send()


def local(
    latents, time_index, fresh_noise, modulation_table, embed_weight, spatial_qkv, spatial_out,
    temporal_qkv, temporal_out, final_weight, spatial_gain, temporal_gain,
):
    gains = jnp.concatenate([spatial_gain, temporal_gain], axis=0).T
    dma = pltpu.SemaphoreType.DMA
    vmem = pl.BlockSpec(memory_space=pltpu.VMEM)
    smem = pl.BlockSpec(memory_space=pltpu.SMEM)
    return pl.pallas_call(
        kernel,
        out_shape=(
            jax.ShapeDtypeStruct(latents.shape, F32),
            jax.ShapeDtypeStruct(latents.shape, F32),
        ),
        in_specs=[vmem, smem] + [vmem] * 9,
        out_specs=(vmem, vmem),
        scratch_shapes=[
            pltpu.VMEM((NS, SHARD, D), BF),
            pltpu.VMEM((2, PATCH, OWN), BF),
            pltpu.VMEM((NS, 2, PATCH, OWN), BF),
            pltpu.VMEM((PATCH, OWN), F32),
            pltpu.VMEM((ROWS + 8, 128), F32),
            pltpu.VMEM((2, HD, TOK), BF),
            pltpu.VMEM((2, TOK, HD), BF),
            pltpu.VMEM((2, HD + 8, TOK), BF),
            pltpu.VMEM((144, TOK), F32),
            pltpu.VMEM((2, 144, TOK), BF),
            pltpu.VMEM((2, D, OWN), BF),
            pltpu.VMEM((16 * NF, WIDE), BF),
            pltpu.VMEM((16 * NF, WIDE), BF),
            pltpu.VMEM((6, ROWS, D), F32),
            pltpu.VMEM((NS, 432, ROWS), F32),
            pltpu.VMEM((D, ROWS), F32),
            pltpu.VMEM((ROWS + 8, 128), F32),
            pltpu.VMEM((NF, 16, 128), F32),
            dma((NS,)),
            dma((NS,)),
            dma((2,)),
            dma((NF,)),
            dma((NF,)),
            dma((14,)),
            dma((14,)),
            dma((14,)),
            dma((14,)),
            dma((2, NS)),
            dma((2, NS)),
            dma((NF,)),
            dma((NF,)),
            dma((NF,)),
            dma((NF,)),
            dma((5,)),
        ],
        compiler_params=pltpu.CompilerParams(
            collective_id=0, has_side_effects=True, vmem_limit_bytes=60 * 1024 * 1024
        ),
    )(
        latents, time_index, fresh_noise, modulation_table.reshape(STEPS * 8, D), embed_weight,
        spatial_qkv, spatial_out, temporal_qkv, temporal_out, final_weight, gains,
    )


def solution(mesh):
    return jax.shard_map(
        local,
        mesh=mesh,
        in_specs=(
            P("frame", None, "space"),
            P("frame"),
            P(None, "space"),
            P(),
            P(),
            P(None, "space"),
            P("space", None),
            P(None, "space"),
            P("space", None),
            P(),
            P(),
            P(),
        ),
        out_specs=(P("frame", None, "space"), P("frame", None, "space")),
        check_vma=False,
    )
```

time: 549 us -> 126 us (0.23)
  waiting for transfers between devices: 348 us -> 0 us
  Pallas kernels: 0 us -> 115 us
  blocking collectives: 89.7 us -> 0 us
  local copies, waits for them, and re-layouts: 51.3 us -> 9.11 us
  matrix products: 30.8 us -> 0 us
  between operations: 14.1 us -> 0.64 us
  other arithmetic: 9.82 us -> 0.7 us
    reduce_scatter x2 -> x0, waiting for transfers between devices: 180 us -> none  [local(): lax.psum_scatter(term.reshape(count, frames_here, width).astype(jnp.bfloa...]
    all_gather x2 -> x0, waiting for transfers between devices: 165 us -> none  [local(): lax.all_gather(ready, 'space', axis=1, tiled=True)]
    pallas_call x0 -> x1, Pallas kernels: none -> 115 us  [local(): pl.pallas_call(kernel, out_shape=(jax.ShapeDtypeStruct(latents.shape, F32...]
    all_to_all x2 -> x0, blocking collectives: 89.7 us -> none  [the longest x1 57.3 us: attend_queue(): lax.all_to_all(packed, 'frame', split_axis=1, concat_axis=0, tiled=True)]
    dot_general x13 -> x0, matrix products: 30.8 us -> none  [the longest x2 9.65 us: project(): jnp.dot(ready.reshape(frames * tokens, width), weight, preferred_element_...]
    reshape x5 -> x0, local copies, waits for them, and re-layouts: 30.3 us -> none  [the longest x2 17.9 us: local(): gathered.reshape(frames_here, frame_count, all_tokens // frame_count, loc...]
    slice x4 -> x0, local copies, waits for them, and re-layouts: 11.3 us -> none  [the longest x1 11.2 us: attend_queue(): split[:, :, :, 2]]
  transfers between devices with their start and end apart: 5 -> 0, of which waited for: 5 -> 0; matrix products, arithmetic and copies ran while one was open for 0% -> 0% of each run, Pallas kernels for 0% -> 0%
where the time goes in v1:
time: 126 us
  Pallas kernels  115 us (91%)
  local copies, waits for them, and re-layouts  9.11 us (7%)
    pallas_call x1, Pallas kernels, local(): pl.pallas_call(kernel, out_shape=(jax.ShapeDtypeStruct(latents.shape, F32...  115 us
    unnamed x7, local copies, waits for them, and re-layouts  8.4 us

profile of v1, /device:TPU:1, one launch (start us, length us, event | category | flops | bytes accessed | tf_op | source)
XLA Modules:
  0.0 125.6 jit_solution(12512573090907297784)
XLA Ops:
  0.6 0.7 pad_maximum_fusion
  1.3 0.7 copy.19
  2.0 0.0 copy-start
  2.0 1.7 %copy.22.final = bf16[1152,16]{1,0:T(8,128)(2,1)} copy(bf16[1152,16]{0,1:T(8,128)(2,1)} %param.21) | data formatting | bytes 73728 | tf_op args[9]
  3.8 2.4 %copy.20.qkv_s = bf16[1152,432]{1,0:T(8,128)(2,1)} copy(bf16[1152,432]{0,1:T(8,128)(2,1)} %param.17) | data formatting | bytes 1990656 | tf_op args[5]
  6.2 0.0 copy-done
  6.2 1.6 %copy.21.qkv_t = bf16[1152,432]{1,0:T(8,128)(2,1)} copy(bf16[1152,432]{0,1:T(8,128)(2,1)S(1)} %copy-done) | data formatting | bytes 1990656 | tf_op args[7]
  7.8 115.2 %shard_map.131 = (f32[2,16,128]{2,1,0:T(8,128)}, f32[2,16,128]{2,1,0:T(8,128)}) custom-call(f32[2,16,128]{2,1,0:T(8,128)} %latents.1, s32[2]{0:T(128)} %steps.1, f32[16,128]{1,0:T(8,128)} %noise.1, bf16[1024,1152]{1,0:T(8,128)(2,1)} %bitcast.2, bf16[16,1152]{1,0:T(8,128)(2,1)} %embed.1, bf16[1152,432]{1,0:T(8,128)(2,1)} %copy.20.qkv_s, ...), custom_call_target="tpu_custom_call" | custom-call | tf_op jit(solution)/shard_map/pallas_call | solution.py:493
  123.0 1.3 %copy.25 = f32[2,16,128]{2,1,0:T(8,128)} copy(f32[2,16,128]{2,1,0:T(8,128)} %get-tuple-element.4) | data formatting | bytes 32768
  124.3 1.3 %copy.26 = f32[2,16,128]{2,1,0:T(8,128)} copy(f32[2,16,128]{2,1,0:T(8,128)} %get-tuple-element.5) | data formatting | bytes 32768
Async XLA Ops:
  2.0 4.2 %copy-start = (bf16[1152,432]{0,1:T(8,128)(2,1)S(1)}, bf16[1152,432]{0,1:T(8,128)(2,1)}, u32[]{:S(2)}) copy-start(bf16[1152,432]{0,1:T(8,128)(2,1)} %param.19) | copy-start | bytes 2985988

commit v2 on v1

--- a/solution.py
+++ b/solution.py
@@ -15,7 +15,8 @@
 OWN = 128
 SUB = 4
 SHARD = 768
-QUARTER = SHARD // 4
+PART = SHARD // 8
+HOPS = 24
 OUT_S, QKV_T, OUT_T = 0, 144, 576
 ROWS = 2 * SUB * NF
 WIDE = 640
@@ -65,16 +66,17 @@
 
 
 def kernel(
-    latents, steps, noise, table, embed, qkv_s, out_s, qkv_t, out_t, final, gains,
+    latents, steps, noise, table_in, embed, qkv_s_in, out_s, qkv_t, out_t, final, gain_s, gain_t,
     velocity, queue,
-    weights, lat_send, lat_all, lat_next, step_rows, qb, kb, vb, att_f, att, att_in, send, recv,
+    table, qkv_s, weights, lat_send, lat_all, lat_next, step_rows, qb, kb, vb, att_f, att, att_in, send, recv,
     mods, proj, att_t, vel_send, vel_recv,
     lat_ssem, lat_rsem, next_sem, step_ssem, step_rsem, dir_ssem, dir_rsem, core_ssem, core_rsem,
-    att_ssem, att_rsem, row_ssem, row_rsem, vel_ssem, vel_rsem, own_sem,
+    att_ssem, att_rsem, row_ssem, row_rsem, vel_ssem, vel_rsem, own_sem, load_sem,
 ):
     f = lax.axis_index("frame")
     s = lax.axis_index("space")
     c = f % 2
+    z = f // 2 % 8
     yl = f // 16
     x = s // 2
     yh = s % 2
@@ -90,6 +92,7 @@
     to_core = (f + step, s)
     to_cross = (lax.rem(f + 16, NF), 2 * x + 1 - yh)
     to_side = (lax.rem(f + 16, NF), s)
+    to_z = (yl * 16 + lax.rem(z + step + 8, 8) * 2 + c, s)
 
     barrier = pltpu.get_barrier_semaphore()
 
@@ -112,18 +115,23 @@
             device_id=target, device_id_type=pl.DeviceIdType.MESH,
         )
 
+    loads = [
+        pltpu.make_async_copy(out_s, weights.at[s, OUT_S:QKV_T, :], load_sem.at[0]),
+        pltpu.make_async_copy(qkv_t, weights.at[s, QKV_T:OUT_T, :], load_sem.at[1]),
+        pltpu.make_async_copy(out_t, weights.at[s, OUT_T : OUT_T + 144, :], load_sem.at[2]),
+        pltpu.make_async_copy(qkv_s_in, qkv_s, load_sem.at[3]),
+        pltpu.make_async_copy(table_in, table, load_sem.at[4]),
+    ]
+    for load in loads:
+        load.start()
     for j in range(2):
         lat_send[j] = latents[j].astype(BF)
-    weights[s, OUT_S:QKV_T, :] = out_s[...]
-    weights[s, OUT_T : OUT_T + 144, :] = out_t[...]
     weights[s, OUT_T + 144 :, :] = jnp.zeros((SHARD - OUT_T - 144, D), BF)
-    eye = (iota((432, 432), 0) == iota((432, 432), 1)).astype(BF)
-    weights[s, QKV_T:OUT_T, :] = dot(eye, qkv_t[...], NT).astype(BF)
     half = iota((8, 128), 0) < SUB
     own_steps = jnp.where(half, steps[0], steps[1]).astype(F32)
     step_rows[pl.ds(pl.multiple_of(f * 8, 8), 8), :] = own_steps
     step_rows[ROWS:, :] = jnp.zeros((8, 128), F32)
-    vel_send[...] = jnp.zeros(vel_send.shape, F32)
+    vel_send[NF:] = jnp.zeros((1, 1, 128), F32)
 
     pl.semaphore_wait(barrier, NF + NS - 1)
 
@@ -150,60 +158,61 @@
     own_lat = pltpu.make_async_copy(lat_send, lat_all.at[s], own_sem.at[0])
     own_lat.start()
 
+    def quarter(m):
+        return lax.rem(yl + m // 2, 2) * 2 + lax.rem(z + m % 2, 2)
+
+    def near(j, who):
+        turn = 1 - 2 * who
+        return (x, lax.rem(x - turn + 4, 4), lax.rem(x + turn + 4, 4), lax.rem(x + 2, 4))[j]
+
     def block(i, who):
-        turn = 1 - 2 * who
-        before = lax.rem(x - turn + 4, 4)
-        after = lax.rem(x + turn + 4, 4)
-        far = lax.rem(x + 2, 4)
-        q = 2 * yl + who
-        r = 2 * (1 - yl) + who
+        j = i % 4
         if i < 4:
-            return before * 2 + yh, (q, 2 * yl + 1 - who, r, 2 * (1 - yl) + 1 - who)[i]
-        if i < 6:
-            return far * 2 + yh, (q, r)[i - 4]
-        across = (x, before, after, far)[(i - 6) % 4] * 2 + 1 - yh
-        return across, (r if i < 10 else q)
-
-    def place(share, quarter):
-        return weights.at[share, pl.ds(pl.multiple_of(quarter * QUARTER, QUARTER), QUARTER), :]
-
-    def hop(i, share, quarter):
-        target = to_x if i < 6 else to_cross if i < 10 else to_side
-        spot = place(share, quarter)
+            return near(1, who) * 2 + yh, quarter(j) * 2, 2
+        if i < 8:
+            return near(3, who) * 2 + yh, quarter(j) * 2 + who, 1
+        return near(j, who) * 2 + 1 - yh, quarter((2, 0, 3, 1)[i // 4 - 2]) * 2 + who, 1
+
+    def hop_source(i):
+        if i < 4:
+            return s, quarter(i) * 2, 2
+        if i < 8:
+            share, part, _ = block(i - 4, c)
+            return share, part + c, 1
+        if i < 12:
+            return near(i - 8, c) * 2 + yh, quarter(0) * 2 + c, 1
+        return block(i - 4 if i < 16 else i - 8, c)
+
+    def place(share, part, count):
+        return weights.at[share, pl.ds(pl.multiple_of(part * PART, PART), PART * count), :]
+
+    def hop(i, spot):
+        target = to_x if i < 8 else to_cross if i < 12 else to_side if i < 16 else to_z
         return push(spot, spot, dir_ssem.at[i], dir_rsem.at[i], target)
 
-    def hop_source(i):
-        q = 2 * yl + c
-        r = 2 * (1 - yl) + c
-        if i < 4:
-            return s, (q, 2 * yl + 1 - c, r, 2 * (1 - yl) + 1 - c)[i]
-        if i < 6:
-            return block((0, 2)[i - 4], c)
-        if i < 10:
-            near = (x, lax.rem(x - step + 4, 4), lax.rem(x + step + 4, 4), lax.rem(x + 2, 4))[i - 6]
-            return near * 2 + yh, q
-        return block(i - 4, c)
-
     def hop_start(i):
-        hop(i, *hop_source(i)).start()
+        hop(i, place(*hop_source(i))).start()
 
     def core_copy(i, who):
         spot = place(*block(i, who))
         return push(spot, spot, core_ssem.at[i], core_rsem.at[i], to_core)
 
-    def take(i, *then):
-        hop(i, *block(i, c)).wait_recv()
-        core_copy(i, c).start()
-        for j in then:
-            hop_start(j)
-
-    def take_core(i, *then):
-        core_copy(i, 1 - c).wait_recv()
-        for j in then:
-            hop_start(j)
-
+    then = {0: (9, 4, 2), 1: (5, 3), 2: (6,), 3: (7,), 4: (11,)}
+    for j in range(4):
+        then[8 + j] = (16 + j, 12 + j)
+        then[12 + j] = (20 + j,)
+
+    def take(*hops):
+        for i in hops:
+            hop(i, place(*block(i, c))).wait_recv()
+            core_copy(i, c).start()
+            for k in then.get(i, ()):
+                hop_start(k)
+
+    for load in loads[:3]:
+        load.wait()
     hop_start(0)
-    hop_start(6)
+    hop_start(8)
     hop_start(1)
 
     @pl.loop(1, NF)
@@ -211,26 +220,26 @@
         step_copy(k, f).start()
 
     next_copy().start()
-    hop_start(2)
-    hop_start(3)
 
     base = embed[...].astype(F32)
     center = base - jnp.mean(base, axis=1, keepdims=True)
     gram = dot(center, center, NT, lax.Precision.HIGHEST) * (1.0 / D)
     gram3 = jnp.concatenate(split3(gram), axis=1)
-    pick_row = iota((8, 8 * STEPS), 0)
-    pick = jnp.zeros((8, 8 * STEPS), jnp.bool_)
-    for j in range(2):
-        for kind in range(2):
-            pick |= (pick_row == 2 * j + kind) & (iota((8, 8 * STEPS), 1) == steps[j] * 8 + kind)
-    own_mods = dot(pick.astype(BF), table[...])
+    eye = (iota((HD, HD), 0) == iota((HD, HD), 1)).astype(F32)
+    gains_s = dot(eye, gain_s[...], NT, lax.Precision.HIGHEST)
+    gains_t = dot(eye, gain_t[...], NT, lax.Precision.HIGHEST)
+    loads[4].wait()
+    slot = iota((16, 8 * STEPS), 1) - iota((16, 8 * STEPS), 0) % 8
+    wanted = jnp.where(iota((16, 8 * STEPS), 0) < 8, steps[0], steps[1]) * 8
+    both_mods = dot((slot == wanted).astype(BF), table[...])
+    own_mods = [both_mods[:8], both_mods[8:]]
     parts = []
     for j in range(2):
-        parts.extend(split2(center * (1.0 + own_mods[2 * j + 1 : 2 * j + 2, :])))
-    parts.extend(split2(own_mods))
+        parts.extend(split2(center * (1.0 + own_mods[j][1:2, :])))
+    parts.append(jnp.concatenate(own_mods, axis=0).astype(BF))
     stack = jnp.concatenate(parts, axis=0)
-    qkv_s_t = dot(eye, qkv_s[...], NT).astype(BF)
-    mixed = dot(qkv_s_t, stack, NT)
+    loads[3].wait()
+    mixed = dot(qkv_s[...], stack, NT)
 
     own_lat.wait()
 
@@ -244,31 +253,28 @@
         spread = jnp.sum(lat32 * dot(gram3, jnp.concatenate([lat] * 3, axis=0)), axis=0, keepdims=True)
         rstd = lax.rsqrt(jnp.maximum(spread, 0.0) + EPS)
         matrix = mixed[:, 32 * j : 32 * j + 16] + mixed[:, 32 * j + 16 : 32 * j + 32]
-        shift = mixed[:, 64 + 2 * j : 65 + 2 * j] + mixed[:, 72 + 2 * j : 73 + 2 * j]
+        shift = mixed[:, 64 + 8 * j : 65 + 8 * j]
         matrix2 = jnp.concatenate(split2(matrix), axis=1)
         projected = dot(matrix2, jnp.concatenate([lat] * 2, axis=0)) * rstd + shift
         ones = (iota((8, TOK), 0) == 0).astype(F32)
         for h in range(2):
             at = h * 3 * HD
-            query = head_norm(projected[at : at + HD], gains[:, 0:1]) * SCORE
-            keys = head_norm(projected[at + HD : at + 2 * HD], gains[:, 1:2])
+            query = head_norm(projected[at : at + HD], gains_s[:, 0:1]) * SCORE
+            keys = head_norm(projected[at + HD : at + 2 * HD], gains_s[:, 1:2])
             values = projected[at + 2 * HD : at + 3 * HD]
             qb[h] = query.astype(BF)
             kb[h] = keys.T.astype(BF)
             vb[h] = jnp.concatenate([values, ones], axis=0).astype(BF)
 
-    def attend_frame(j):
+    def attend_head(h):
         chunk = 256
 
-        @pl.loop(0, 2 * TOK // chunk)
+        @pl.loop(0, TOK // chunk)
         def _(i):
-            h = i // (TOK // chunk)
-            columns = pl.ds(pl.multiple_of(i % (TOK // chunk) * chunk, chunk), chunk)
+            columns = pl.ds(pl.multiple_of(i * chunk, chunk), chunk)
             scores = dot(kb[h], qb[h, :, columns])
             weighted = dot(vb[h], jnp.exp2(scores).astype(BF))
-            att_f[pl.ds(pl.multiple_of(h * HD, 8), HD), columns] = weighted[:HD] / weighted[HD : HD + 1]
-
-        att[j] = att_f[...].astype(BF)
+            att_f[h * HD : (h + 1) * HD, columns] = weighted[:HD] / weighted[HD : HD + 1]
 
     def share_rows(share):
         return pl.ds(pl.multiple_of(share * 144, 16), 144)
@@ -297,19 +303,21 @@
 
     for j in range(2):
         project_frame(j)
-        attend_frame(j)
+        if j == 0:
+            take(0, 8)
+            core_copy(0, 1 - c).wait_recv()
+            hop_start(10)
+        attend_head(0)
+        take(*((1, 16) if j == 0 else (17, 20, 10, 2)))
+        attend_head(1)
+        att[j] = att_f[...].astype(BF)
 
         @pl.loop(1, NS)
         def _(k):
             att_copy(j, k).start()
 
         att_own(j).start()
-        if j == 0:
-            take(0, 4, 7)
-        else:
-            take(6, 10)
-            take(1)
-            take_core(1, 8)
+        take(*((12, 9, 4) if j == 0 else (13, 5, 11)))
 
     for j in range(2):
         att_own(j).wait()
@@ -317,6 +325,8 @@
         @pl.loop(1, NS)
         def _(k):
             att_wait(j, k)
+
+    take(18, 14, 3)
 
     row, column = iota((16 * NF, 2 * OWN), 0), iota((16 * NF, 2 * OWN), 1)
     matching = column == row % 8 // SUB * OWN + row // 16 * SUB + row % SUB
@@ -351,6 +361,8 @@
     own_copy = pltpu.make_async_copy(send.at[own_rows, :], recv.at[own_rows, :], own_sem.at[3])
     own_copy.start()
 
+    take(21, 19, 6)
+
     @pl.loop(1, NF)
     def _(k):
         step_copy(k, frame_peer(k)).wait_recv()
@@ -360,27 +372,15 @@
     for kind in range(6):
         mods[kind] = dot((wanted + (kind + 2.0) == slots).astype(BF), table[...])
 
-    take(2, 5)
-    take(3)
-    take(4, 9)
-    take(7, 11)
-    take(5)
-    take(10)
-    take(8, 12)
-    take(11)
-    take(9, 13)
-
+    take(15, 22, 7, 23)
     own_copy.wait()
 
     @pl.loop(1, NF)
     def _(k):
         row_wait(k)
 
-    take(12)
-    take(13)
-
-    for i in (0, 2, 3, 4, 5, 6, 7, 8, 9, 10, 11, 12, 13):
-        take_core(i)
+    for i in range(1, HOPS):
+        core_copy(i, 1 - c).wait_recv()
 
     row, column = iota((ROWS, 16 * NF), 0), iota((ROWS, 16 * NF), 1)
     halves = [
@@ -399,34 +399,38 @@
     same = iota((ROWS, ROWS), 0) % SUB == iota((ROWS, ROWS), 1) % SUB
     ones = (iota((8, ROWS), 0) == 0).astype(F32)
 
-    @pl.loop(0, 2 * NS)
+    @pl.loop(0, NS // 2)
     def _(i):
-        share, at = i // 2, pl.multiple_of(i % 2 * 3 * HD, 8)
-        query = head_norm(proj[share, pl.ds(at, HD), :], gains[:, 2:3]) * SCORE
-        keys = head_norm(proj[share, pl.ds(at + HD, HD), :], gains[:, 3:4])
-        values = jnp.concatenate([proj[share, pl.ds(at + 2 * HD, HD), :], ones], axis=0).astype(BF)
-        scores = dot(keys.T.astype(BF), query.astype(BF))
-        weighted = dot(values, jnp.where(same, jnp.exp2(scores), 0.0).astype(BF))
-        att_t[pl.ds(pl.multiple_of(i * HD, 8), HD), :] = weighted[:HD] / weighted[HD : HD + 1]
+        for n in range(4):
+            share, at = 2 * i + n // 2, n % 2 * 3 * HD
+            query = head_norm(proj[share, at : at + HD, :], gains_t[:, 0:1]) * SCORE
+            keys = head_norm(proj[share, at + HD : at + 2 * HD, :], gains_t[:, 1:2])
+            values = jnp.concatenate([proj[share, at + 2 * HD : at + 3 * HD, :], ones], axis=0).astype(BF)
+            scores = dot(keys.T.astype(BF), query.astype(BF))
+            weighted = dot(values, jnp.where(same, jnp.exp2(scores), 0.0).astype(BF))
+            rows = pl.ds(pl.multiple_of((4 * i + n) * HD, 8), HD)
+            att_t[rows, :] = weighted[:HD] / weighted[HD : HD + 1]
 
     output = jnp.zeros((ROWS, D), F32)
     for i in range(NS):
         output += dot(att_t[144 * i : 144 * i + 144, :].T.astype(BF), weights[i, OUT_T : OUT_T + 144, :])
     hidden += mods[3] * output
     ready = (layer_norm(hidden) * (1.0 + mods[5]) + mods[4]).astype(BF)
-    vel_send[0:ROWS, 0:PATCH] = dot(ready, final[...])
+    wide = dot(ready, jnp.concatenate([final[...]] * 8, axis=0), NT)
+    wide = jnp.where(iota((ROWS, 128), 0) % 8 == iota((ROWS, 128), 1) // PATCH, wide, 0.0)
+    vel_send[0:NF] = jnp.sum(wide.reshape(NF, 8, 128), axis=1, keepdims=True)
 
     def vel_copy(k):
         peer = frame_peer(k)
         return push(
-            vel_send.at[pl.ds(pl.multiple_of(peer * 8, 8), 16), :], vel_recv.at[f],
+            vel_send.at[pl.ds(peer, 2)], vel_recv.at[f],
             vel_ssem.at[k], vel_rsem.at[f], (peer, s),
         )
 
     def vel_wait(k):
         origin = frame_peer(k)
         push(
-            vel_send.at[pl.ds(pl.multiple_of(origin * 8, 8), 16), :], vel_recv.at[origin],
+            vel_send.at[pl.ds(origin, 2)], vel_recv.at[origin],
             vel_ssem.at[k], vel_rsem.at[origin], (origin, s),
         ).wait_recv()
 
@@ -435,7 +439,7 @@
         vel_copy(k).start()
 
     own_vel = pltpu.make_async_copy(
-        vel_send.at[pl.ds(pl.multiple_of(f * 8, 8), 16), :], vel_recv.at[f], own_sem.at[4]
+        vel_send.at[pl.ds(f, 2)], vel_recv.at[f], own_sem.at[4]
     )
     own_vel.start()
     next_copy().wait_recv()
@@ -445,13 +449,16 @@
     def _(k):
         vel_wait(k)
 
-    turned = vel_recv[...].reshape(16 * NF, 128).T[0:PATCH, :]
-    turned3 = jnp.concatenate(split3(turned), axis=0)
-    row, column = iota((16 * NF, OWN), 0), iota((16 * NF, OWN), 1)
+    turned = [vel_recv[:, i, 0, :].T for i in range(2)]
+    row, column = iota((NF, OWN), 0), iota((NF, OWN), 1)
     updated = []
     for j in range(3):
-        spread = dot(turned3, (row == column // SUB * 16 + j * SUB + column % SUB).astype(BF))
-        found = spread[0:16] + spread[16:32] + spread[32:48]
+        found = jnp.zeros((PATCH, OWN), F32)
+        for t in range(SUB):
+            at = (j % 2 * SUB + t) * PATCH
+            mine = jnp.concatenate(split3(turned[j // 2][at : at + PATCH]), axis=0)
+            spread = dot(mine, (column == SUB * row + t).astype(BF))
+            found += spread[0:16] + spread[16:32] + spread[32:48]
         index = step_rows[pl.ds(f * 8 + j * SUB, 1), :]
         size = level(index + 1.0) - level(index)
         if j < 2:
@@ -477,8 +484,8 @@
         vel_copy(k).wait_send()
 
     next_copy().wait_send()
-    for i in range(14):
-        hop(i, *hop_source(i)).wait_send()
+    for i in range(HOPS):
+        hop(i, place(*hop_source(i))).wait_send()
         core_copy(i, c).wait_send()
 
 
@@ -486,9 +493,9 @@
     latents, time_index, fresh_noise, modulation_table, embed_weight, spatial_qkv, spatial_out,
     temporal_qkv, temporal_out, final_weight, spatial_gain, temporal_gain,
 ):
-    gains = jnp.concatenate([spatial_gain, temporal_gain], axis=0).T
     dma = pltpu.SemaphoreType.DMA
     vmem = pl.BlockSpec(memory_space=pltpu.VMEM)
+    hbm = pl.BlockSpec(memory_space=pl.ANY)
     smem = pl.BlockSpec(memory_space=pltpu.SMEM)
     return pl.pallas_call(
         kernel,
@@ -496,9 +503,11 @@
             jax.ShapeDtypeStruct(latents.shape, F32),
             jax.ShapeDtypeStruct(latents.shape, F32),
         ),
-        in_specs=[vmem, smem] + [vmem] * 9,
+        in_specs=[vmem, smem, vmem, hbm, vmem, hbm, hbm, hbm, hbm, vmem, vmem, vmem],
         out_specs=(vmem, vmem),
         scratch_shapes=[
+            pltpu.VMEM((8 * STEPS, D), BF),
+            pltpu.VMEM((432, D), BF),
             pltpu.VMEM((NS, SHARD, D), BF),
             pltpu.VMEM((2, PATCH, OWN), BF),
             pltpu.VMEM((NS, 2, PATCH, OWN), BF),
@@ -515,17 +524,17 @@
             pltpu.VMEM((6, ROWS, D), F32),
             pltpu.VMEM((NS, 432, ROWS), F32),
             pltpu.VMEM((D, ROWS), F32),
-            pltpu.VMEM((ROWS + 8, 128), F32),
-            pltpu.VMEM((NF, 16, 128), F32),
+            pltpu.VMEM((NF + 1, 1, 128), F32),
+            pltpu.VMEM((NF, 2, 1, 128), F32),
             dma((NS,)),
             dma((NS,)),
             dma((2,)),
             dma((NF,)),
             dma((NF,)),
-            dma((14,)),
-            dma((14,)),
-            dma((14,)),
-            dma((14,)),
+            dma((HOPS,)),
+            dma((HOPS,)),
+            dma((HOPS,)),
+            dma((HOPS,)),
             dma((2, NS)),
             dma((2, NS)),
             dma((NF,)),
@@ -533,13 +542,14 @@
             dma((NF,)),
             dma((NF,)),
             dma((5,)),
+            dma((5,)),
         ],
         compiler_params=pltpu.CompilerParams(
             collective_id=0, has_side_effects=True, vmem_limit_bytes=60 * 1024 * 1024
         ),
     )(
         latents, time_index, fresh_noise, modulation_table.reshape(STEPS * 8, D), embed_weight,
-        spatial_qkv, spatial_out, temporal_qkv, temporal_out, final_weight, gains,
+        spatial_qkv.T, spatial_out, temporal_qkv.T, temporal_out, final_weight.T, spatial_gain, temporal_gain,
     )
 
 

time: 126 us -> 95.9 us (0.76)
  Pallas kernels: 115 us -> 92.3 us
  local copies, waits for them, and re-layouts: 9.11 us -> 2.65 us
    pallas_call x1, Pallas kernels: 115 us -> 92.3 us  [local(): pl.pallas_call(kernel, out_shape=(jax.ShapeDtypeStruct(latents.shape, F32...]
    unnamed x7 -> x2, local copies, waits for them, and re-layouts: 8.4 us -> 2.65 us
where the time goes in v2:
time: 95.9 us; the launch traced here: 95.6 us
  Pallas kernels  92.3 us (96%)
  local copies, waits for them, and re-layouts  2.65 us (3%)
    pallas_call x1, Pallas kernels, local(): pl.pallas_call(kernel, out_shape=(jax.ShapeDtypeStruct(latents.shape, F32...  92.3 us
    unnamed x2, local copies, waits for them, and re-layouts  2.65 us

profile of v2, /device:TPU:1, one launch (start us, length us, event | category | flops | bytes accessed | tf_op | source)
XLA Modules:
  0.0 95.6 jit_solution(7565682933847360015)
XLA Ops:
  0.6 92.3 %shard_map.131 = (f32[2,16,128]{2,1,0:T(8,128)}, f32[2,16,128]{2,1,0:T(8,128)}) custom-call(f32[2,16,128]{2,1,0:T(8,128)} %latents.1, s32[2]{0:T(128)} %steps.1, f32[16,128]{1,0:T(8,128)} %noise.1, bf16[1024,1152]{1,0:T(8,128)(2,1)} %bitcast.4, bf16[16,1152]{1,0:T(8,128)(2,1)} %embed.1, bf16[432,1152]{1,0:T(8,128)(2,1)} %bitcast.5, bf16[144,1152]{1,0:T(8,128)(2,1)} %out_s.1, ...), custom_call_target="tpu_custom_call" | custom-call | tf_op jit(solution)/shard_map/pallas_call | solution.py:500
  93.0 1.3 %copy.16 = f32[2,16,128]{2,1,0:T(8,128)} copy(f32[2,16,128]{2,1,0:T(8,128)} %get-tuple-element.4) | data formatting | bytes 32768
  94.3 1.3 %copy.17 = f32[2,16,128]{2,1,0:T(8,128)} copy(f32[2,16,128]{2,1,0:T(8,128)} %get-tuple-element.5) | data formatting | bytes 32768

commit v3 on v2

--- a/solution.py
+++ b/solution.py
@@ -67,7 +67,7 @@
 
 def kernel(
     latents, steps, noise, table_in, embed, qkv_s_in, out_s, qkv_t, out_t, final, gain_s, gain_t,
-    velocity, queue,
+    result,
     table, qkv_s, weights, lat_send, lat_all, lat_next, step_rows, qb, kb, vb, att_f, att, att_in, send, recv,
     mods, proj, att_t, vel_send, vel_recv,
     lat_ssem, lat_rsem, next_sem, step_ssem, step_rsem, dir_ssem, dir_rsem, core_ssem, core_rsem,
@@ -204,6 +204,10 @@
 
     def take(*hops):
         for i in hops:
+            if i is None:
+                core_copy(0, 1 - c).wait_recv()
+                hop_start(10)
+                continue
             hop(i, place(*block(i, c))).wait_recv()
             core_copy(i, c).start()
             for k in then.get(i, ()):
@@ -267,7 +271,7 @@
             vb[h] = jnp.concatenate([values, ones], axis=0).astype(BF)
 
     def attend_head(h):
-        chunk = 256
+        chunk = 512
 
         @pl.loop(0, TOK // chunk)
         def _(i):
@@ -301,14 +305,13 @@
             att.at[j, :, share_columns(s)], att_in.at[j, share_rows(s), :], own_sem.at[1 + j]
         )
 
+    stops = iter(((0, 8, None), (1, 16), (12, 9, 4), (17, 20), (10, 2), (13, 5, 11), (18, 14), (3, 21), (19, 6, 15, 22), (7, 23)))
     for j in range(2):
+        take(*next(stops))
         project_frame(j)
-        if j == 0:
-            take(0, 8)
-            core_copy(0, 1 - c).wait_recv()
-            hop_start(10)
+        take(*next(stops))
         attend_head(0)
-        take(*((1, 16) if j == 0 else (17, 20, 10, 2)))
+        take(*next(stops))
         attend_head(1)
         att[j] = att_f[...].astype(BF)
 
@@ -317,7 +320,8 @@
             att_copy(j, k).start()
 
         att_own(j).start()
-        take(*((12, 9, 4) if j == 0 else (13, 5, 11)))
+
+    take(*next(stops))
 
     for j in range(2):
         att_own(j).wait()
@@ -326,7 +330,7 @@
         def _(k):
             att_wait(j, k)
 
-    take(18, 14, 3)
+    take(*next(stops))
 
     row, column = iota((16 * NF, 2 * OWN), 0), iota((16 * NF, 2 * OWN), 1)
     matching = column == row % 8 // SUB * OWN + row // 16 * SUB + row % SUB
@@ -361,7 +365,7 @@
     own_copy = pltpu.make_async_copy(send.at[own_rows, :], recv.at[own_rows, :], own_sem.at[3])
     own_copy.start()
 
-    take(21, 19, 6)
+    take(*next(stops))
 
     @pl.loop(1, NF)
     def _(k):
@@ -372,21 +376,21 @@
     for kind in range(6):
         mods[kind] = dot((wanted + (kind + 2.0) == slots).astype(BF), table[...])
 
-    take(15, 22, 7, 23)
+    take(*next(stops))
     own_copy.wait()
 
     @pl.loop(1, NF)
     def _(k):
         row_wait(k)
-
-    for i in range(1, HOPS):
-        core_copy(i, 1 - c).wait_recv()
 
     row, column = iota((ROWS, 16 * NF), 0), iota((ROWS, 16 * NF), 1)
     halves = [
         dot((column == row // 8 * 16 + h * 8 + row % 8).astype(BF), recv[...]) for h in range(2)
     ]
     hidden = dot(halves[0][:, D // 2 : D // 2 + PATCH].astype(BF), embed[...])
+    for i in range(1, HOPS):
+        core_copy(i, 1 - c).wait_recv()
+
     output = jnp.zeros((ROWS, D), F32)
     for i in range(NS):
         at = i % 4 * 144
@@ -462,10 +466,10 @@
         index = step_rows[pl.ds(f * 8 + j * SUB, 1), :]
         size = level(index + 1.0) - level(index)
         if j < 2:
-            velocity[j] = found
+            result[j] = found
         updated.append((latents[j] if j < 2 else lat_next[...]) - size * found)
-    queue[0] = updated[1]
-    queue[1] = jnp.where(f == NF - 1, noise[...], updated[2])
+    result[2] = updated[1]
+    result[3] = jnp.where(f == NF - 1, noise[...], updated[2])
 
     for j in range(2):
 
@@ -497,14 +501,11 @@
     vmem = pl.BlockSpec(memory_space=pltpu.VMEM)
     hbm = pl.BlockSpec(memory_space=pl.ANY)
     smem = pl.BlockSpec(memory_space=pltpu.SMEM)
-    return pl.pallas_call(
+    result = pl.pallas_call(
         kernel,
-        out_shape=(
-            jax.ShapeDtypeStruct(latents.shape, F32),
-            jax.ShapeDtypeStruct(latents.shape, F32),
-        ),
+        out_shape=jax.ShapeDtypeStruct((4, PATCH, OWN), F32),
         in_specs=[vmem, smem, vmem, hbm, vmem, hbm, hbm, hbm, hbm, vmem, vmem, vmem],
-        out_specs=(vmem, vmem),
+        out_specs=vmem,
         scratch_shapes=[
             pltpu.VMEM((8 * STEPS, D), BF),
             pltpu.VMEM((432, D), BF),
@@ -551,6 +552,7 @@
         latents, time_index, fresh_noise, modulation_table.reshape(STEPS * 8, D), embed_weight,
         spatial_qkv.T, spatial_out, temporal_qkv.T, temporal_out, final_weight.T, spatial_gain, temporal_gain,
     )
+    return result[:2], result[2:]
 
 
 def solution(mesh):

time: 95.9 us -> 91.9 us (0.958)
  Pallas kernels: 92.3 us -> 89.7 us
  local copies, waits for them, and re-layouts: 2.65 us -> 1.35 us
    unnamed x2 -> x0, local copies, waits for them, and re-layouts: 2.65 us -> none
    pallas_call x1, Pallas kernels: 92.3 us -> 89.7 us  [local(): pl.pallas_call(kernel, out_shape=jax.ShapeDtypeStruct((4, PATCH, OWN), F3...]
    slice x0 -> x1, local copies, waits for them, and re-layouts: none -> 1.35 us  [local(): return (result[:2], result[2:])]
where the time goes in v3:
time: 91.9 us; the launch traced here: 91.7 us
  Pallas kernels  89.7 us (98%)
  local copies, waits for them, and re-layouts  1.35 us (1%)
    pallas_call x1, Pallas kernels, local(): pl.pallas_call(kernel, out_shape=jax.ShapeDtypeStruct((4, PATCH, OWN), F3...  89.7 us

profile of v3, /device:TPU:1, one launch (start us, length us, event | category | flops | bytes accessed | tf_op | source)
XLA Modules:
  0.0 91.7 jit_solution(3807502220382459293)
XLA Ops:
  0.6 89.7 %shard_map.131 = f32[4,16,128]{2,1,0:T(8,128)} custom-call(f32[2,16,128]{2,1,0:T(8,128)} %latents.1, s32[2]{0:T(128)} %steps.1, f32[16,128]{1,0:T(8,128)} %noise.1, bf16[1024,1152]{1,0:T(8,128)(2,1)} %bitcast.4, bf16[16,1152]{1,0:T(8,128)(2,1)} %embed.1, bf16[432,1152]{1,0:T(8,128)(2,1)} %bitcast.5, bf16[144,1152]{1,0:T(8,128)(2,1)} %out_s.1, ...), custom_call_target="tpu_custom_call" | custom-call | tf_op jit(solution)/shard_map/pallas_call | solution.py:504
  90.3 1.3 %fusion = (f32[2,16,128]{2,1,0:T(8,128)}, f32[2,16,128]{2,1,0:T(8,128)}) fusion(f32[4,16,128]{2,1,0:T(8,128)} %shard_map.131), kind=kLoop, calls=%fused_computation | loop fusion | bytes 65536 | tf_op jit(solution)/shard_map/slice | solution.py:555
